TPU v7x, 32 devices: a whole 2x2x4 slice. The times are simulated.
32 devices in a mesh: groups: 2 (over y), dp: 8 (over z, x), fsdp: 2 (over core).
Axes of the slice: x: 2, y: 2, z: 4, core: 2. Of those that a mesh axis runs over, the one named last changes fastest.
Arguments:
- layer_input: bfloat16 [4096, 8192], P(('groups', 'dp'), 'fsdp'), parts along dimension 0, may hold values from -6 to 6
- w_value: bfloat16 [8192, 128], P('fsdp', 'dp'), may hold values from -0.0625 to 0.0625
- queries: bfloat16 [4096, 1024], P(('groups', 'dp'), 'fsdp'), parts along dimension 0, may hold values from -16 to 16
- keys: bfloat16 [4096, 128], P(('groups', 'dp')), parts along dimension 0, may hold values from -16 to 16
- grad_out: bfloat16 [4096, 1024], P(('groups', 'dp'), 'fsdp'), parts along dimension 0, may hold values from -6 to 6
- doc_lengths: int32 [8], P('groups'), parts along dimension 0, may hold values from 1 to 768, 2048 in all
- prefix_spans: int32 [8], P('groups'), parts along dimension 0, may hold values from 1 to 768
Outputs:
- grad_input: bfloat16 [4096, 8192], P(('groups', 'dp'), 'fsdp'), parts along dimension 0
- grad_queries: bfloat16 [4096, 1024], P(('groups', 'dp'), 'fsdp'), parts along dimension 0
- grad_keys: bfloat16 [4096, 128], P(('groups', 'dp')), parts along dimension 0
- grad_weight: float32 [16384, 128], P(('groups', 'fsdp'), 'dp'), parts along dimension 0
There are 2 independent parts, one for each index of `groups`. A program takes and returns all parts, laid end to end along the dimension named above; an argument that names none is the same for every part. Nothing has to cross between parts.
Inputs may be any that keep to these rules, and one draw needn't show every extreme that they name: `doc_lengths`: the lengths sum to 2048 and one of them equals 768.
All inputs are finite; a program needn't handle non-finite values.
Results may differ from a plain program's by a relative error of at most 0.0065.
Values may be sent and summed in bfloat16 or wider, within the bound.
No kernel may reach another device: no remote copies, remote signals or barrier semaphores. Data moves between devices by JAX's collectives and lax.ppermute only.
A program may use at most 128 MiB of HBM per device.

v0:
```python
import jax
import jax.numpy as jnp
from jax import lax
from jax.sharding import PartitionSpec as P

SPAN = 3


NEGATIVE = -1e30


def passed_along(value, axis, steps):
    count = lax.axis_size(axis)
    leading, last = (max(0, -steps), min(count, count - steps))
    return lax.ppermute(value, axis, [(source, source + steps) for source in range(leading, last)])


def doc_tables(doc_lengths, prefix_spans):
    ends = jnp.cumsum(doc_lengths)
    starts = ends - doc_lengths
    prefix_end = starts + jnp.minimum(prefix_spans, doc_lengths)
    return (ends, prefix_end)


def locate(positions, ends, prefix_end):
    document = jnp.sum((positions[:, None] >= ends[None, :]).astype(jnp.int32), axis=1)
    members = document[:, None] == jnp.arange(ends.shape[0], dtype=jnp.int32)[None, :]
    bound = jnp.sum(jnp.where(members, prefix_end[None, :], 0), axis=1)
    return (document, bound)


def visible_mask(query_positions, key_positions, ends, prefix_end, total_rows):
    query_doc, query_bound = locate(query_positions, ends, prefix_end)
    key_doc, unused_bound = locate(key_positions, ends, prefix_end)
    inside = (key_positions >= 0) & (key_positions < total_rows)
    same_doc = query_doc[:, None] == key_doc[None, :]
    allowed = (key_positions[None, :] <= query_positions[:, None]) | (
        key_positions[None, :] < query_bound[:, None]
    )
    return same_doc & allowed & inside[None, :]


def score_block(query_rows, grad_rows, key_block, value_block):
    scores = jnp.einsum("thd,kd->htk", query_rows, key_block, preferred_element_type=jnp.float32)
    grad_probs = jnp.einsum(
        "thd,kd->htk", grad_rows, value_block, preferred_element_type=jnp.float32
    )
    return (scores, grad_probs)


def grad_block(grad_scores, rounded, query_rows, grad_rows, key_block):
    grad_query = jnp.einsum(
        "htk,kd->thd", grad_scores, key_block, preferred_element_type=jnp.float32
    )
    grad_key = jnp.einsum(
        "htk,thd->kd", grad_scores, query_rows, preferred_element_type=jnp.float32
    )
    grad_value = jnp.einsum("htk,thd->kd", rounded, grad_rows, preferred_element_type=jnp.float32)
    return (grad_query, jnp.concatenate([grad_key, grad_value], axis=1))


def body(layer_input, w_value, queries, keys, grad_out, doc_lengths, prefix_spans):
    rows_here = layer_input.shape[0]
    head_size = keys.shape[1]
    local_heads = queries.shape[1] // head_size
    dp_count = lax.axis_size("dp")
    my_index = lax.axis_index("dp")
    span_dev = SPAN
    window_blocks = 2 * span_dev + 1
    full_weight = lax.all_gather(w_value, "dp", axis=1, tiled=True)
    value_part = jnp.dot(layer_input, full_weight, preferred_element_type=jnp.float32)
    value_rows = lax.psum(value_part, "fsdp").astype(jnp.bfloat16)
    pairs = jnp.concatenate([keys, value_rows], axis=1)
    behind = [passed_along(pairs, "dp", distance) for distance in range(span_dev, 0, -1)]
    ahead = [passed_along(pairs, "dp", -distance) for distance in range(1, span_dev + 1)]
    window = jnp.stack(behind + [pairs] + ahead)
    ends, prefix_end = doc_tables(doc_lengths, prefix_spans)
    query_positions = my_index * rows_here + jnp.arange(rows_here, dtype=jnp.int32)
    key_positions = (my_index - span_dev) * rows_here + jnp.arange(
        window_blocks * rows_here, dtype=jnp.int32
    )
    visible = visible_mask(query_positions, key_positions, ends, prefix_end, rows_here * dp_count)
    query_rows = queries.reshape(rows_here, local_heads, head_size)
    grad_rows = grad_out.reshape(rows_here, local_heads, head_size)
    key_window = window[:, :, :head_size]
    value_window = window[:, :, head_size:]
    key_flat = key_window.reshape(window_blocks * rows_here, head_size)
    value_flat = value_window.reshape(window_blocks * rows_here, head_size)
    scaling = 1.0 / jnp.sqrt(jnp.float32(head_size))
    scores, grad_probs = score_block(query_rows, grad_rows, key_flat, value_flat)
    scores = jnp.where(visible[None], scores * scaling, NEGATIVE)
    peak = jnp.max(scores, axis=2, keepdims=True)
    expos = jnp.exp(scores - peak)
    attention = expos / jnp.sum(expos, axis=2, keepdims=True)
    rounded = attention.astype(jnp.bfloat16)
    delta = jnp.sum(attention * grad_probs, axis=2, keepdims=True)
    grad_scores = (attention * (grad_probs - delta) * scaling).astype(jnp.bfloat16)
    grad_query, partial_value = grad_block(grad_scores, rounded, query_rows, grad_rows, key_flat)
    partial_value = partial_value.reshape(window_blocks, rows_here, 2 * head_size)
    grad_queries = grad_query.reshape(rows_here, local_heads * head_size).astype(jnp.bfloat16)
    gathered = partial_value[span_dev]
    for distance in range(1, span_dev + 1):
        gathered = gathered + passed_along(partial_value[span_dev - distance], "dp", -distance)
        gathered = gathered + passed_along(partial_value[span_dev + distance], "dp", distance)
    summed = lax.psum(gathered, "fsdp")
    grad_keys = summed[:, :head_size].astype(jnp.bfloat16)
    grad_value = summed[:, head_size:].astype(jnp.bfloat16)
    grad_input = lax.dot_general(
        grad_value, full_weight, (((1,), (1,)), ((), ())), preferred_element_type=jnp.float32
    ).astype(jnp.bfloat16)
    grad_weight = lax.psum_scatter(
        lax.dot_general(
            grad_value, layer_input, (((0,), (0,)), ((), ())), preferred_element_type=jnp.float32
        ),
        "dp",
        scatter_dimension=0,
        tiled=True,
    ).T
    return (grad_input, grad_queries, grad_keys, grad_weight)


def solution(mesh):
    in_specs = (
        P(("groups", "dp"), "fsdp"),
        P("fsdp", "dp"),
        P(("groups", "dp"), "fsdp"),
        P(("groups", "dp"), None),
        P(("groups", "dp"), "fsdp"),
        P("groups"),
        P("groups"),
    )
    out_specs = (
        P(("groups", "dp"), "fsdp"),
        P(("groups", "dp"), "fsdp"),
        P(("groups", "dp"), None),
        P(("groups", "fsdp"), "dp"),
    )
    return jax.shard_map(body, mesh=mesh, in_specs=in_specs, out_specs=out_specs, check_vma=False)
```

profile of v0, /device:TPU:0, one launch (start us, length us, event | category | flops | bytes accessed | tf_op | source)
XLA Modules:
  0.0 224.2 jit_solution(15651766450091252104)
XLA Ops:
  9.8 43.3 %all-gather.2.cloned.1.call-done = bf16[4096,128]{0,1:T(8,128)(2,1)} async-done(((bf16[4096,16]{0,1:T(8,128)(2,1)}), bf16[4096,128]{0,1:T(8,128)(2,1)}) %all-gather.2.cloned.1.call-update) | async-done | bytes 1048592 | tf_op jit(solution)/shard_map/all_gather | solution.py:70
  53.0 1.9 fusion.44
  55.0 3.8 %all-reduce.2 = bf16[256,128]{1,0:T(8,128)(2,1)S(1)} all-reduce(f32[256,128]{1,0:T(8,128)S(1)} %fusion.44), channel_id=1, replica_groups=mesh['groups'=2,'dp'=8,'fsdp'=2] {'fsdp'}, use_global_device_ids=true, to_apply=%region_4.5 | all-reduce | flops 32768 | bytes 196608 | tf_op jit(solution)/shard_map/psum | solution.py:72
  59.7 3.1 %collective-permute-start = (bf16[256,256]{1,0:T(8,128)(2,1)S(1)}, bf16[256,256]{1,0:T(8,128)(2,1)}, u32[]{:S(2)}, u32[]{:S(2)}) collective-permute-start(bf16[256,256]{1,0:T(8,128)(2,1)S(1)} %pad_maximum_fusion.1), channel_id=1, source_target_pairs={{0,6},{2,8},{4,10},{6,12},{8,14},{1,7},{3,9},{5,11},{7,13},{9,15},... | collective-permute-start | bytes 393224 | tf_op jit(solution)/shard_map/ppermute | solution.py:15
  62.7 1.6 and_and_fusion
  64.3 1.1 copy.36
  65.4 1.1 copy.37
  66.5 1.3 collective-permute-start.4
  67.8 1.3 collective-permute-start.3
  69.1 1.3 collective-permute-start.5
  70.4 4.6 %collective-permute-start.2 = (bf16[256,256]{1,0:T(8,128)(2,1)S(1)}, bf16[256,256]{1,0:T(8,128)(2,1)S(1)}, u32[]{:S(2)}, u32[]{:S(2)}) collective-permute-start(bf16[256,256]{1,0:T(8,128)(2,1)S(1)} %pad_maximum_fusion.1), channel_id=1, source_target_pairs={{0,2},{2,4},{4,6},{6,8},{8,10},{10,12},{12,14},{1,3},{3,5},{5,7},{... | collective-permute-start | bytes 393224 | tf_op jit(solution)/shard_map/ppermute | solution.py:15
  75.0 5.2 %collective-permute-start.1 = (bf16[256,256]{1,0:T(8,128)(2,1)S(1)}, bf16[256,256]{1,0:T(8,128)(2,1)S(1)}, u32[]{:S(2)}, u32[]{:S(2)}) collective-permute-start(bf16[256,256]{1,0:T(8,128)(2,1)S(1)} %pad_maximum_fusion.1), channel_id=1, source_target_pairs={{0,4},{2,6},{4,8},{6,10},{8,12},{10,14},{1,5},{3,7},{5,9},{7,11},{... | collective-permute-start | bytes 393224 | tf_op jit(solution)/shard_map/ppermute | solution.py:15
  81.1 1.6 collective-permute-done.1
  83.8 4.1 %fusion.45 = f32[1792,256,4]{1,0,2:T(8,128)} fusion(bf16[1792,128,1]{1,0,2:T(8,128)(2,1)S(1)} %bitcast.86, bf16[256,4,128]{0,2,1:T(8,128)(2,1)S(1)} %bitcast.87), kind=kOutput, calls=%fused_computation.78 | convolution fusion | flops 469762048 | bytes 8060928 | tf_op jit(solution)/shard_map/thd,kd->htk/dot_general | solution.py:45
  87.9 5.6 %fusion.43 = (f32[4,256]{1,0:T(4,128)S(1)}, f32[4,256,1792]{1,2,0:T(8,128)}) fusion(pred[256,1792]{0,1:T(8,128)(4,1)S(1)} %and_and_fusion, bf16[1792,128,1]{1,0,2:T(8,128)(2,1)S(1)} %bitcast.89, bf16[256,4,128]{0,2,1:T(8,128)(2,1)S(1)} %bitcast.91), kind=kOutput, calls=%fused_computation.76 | convolution fusion | flops 477103872 | bytes 8523776 | tf_op jit(solution)/shard_map/sub | solution.py:93
  93.5 4.4 %fusion.14 = f32[1792,128]{0,1:T(8,128)S(1)} fusion(bf16[256,4,128]{0,2,1:T(8,128)(2,1)S(1)} %bitcast.88, f32[4,256,1792]{1,2,0:T(8,128)} %get-tuple-element.21, f32[4,256]{1,0:T(4,128)S(1)} %get-tuple-element.20), kind=kOutput, calls=%fused_computation.32 | convolution fusion | flops 473432064 | bytes 8523776 | tf_op jit(solution)/shard_map/htk,thd->kd/dot_general | solution.py:58
  98.0 11.6 %fusion.17 = f32[1792,128]{0,1:T(8,128)} fusion(bf16[256,4,128]{0,2,1:T(8,128)(2,1)S(1)} %bitcast.92, f32[1792,256,4]{1,0,2:T(8,128)} %fusion.45, f32[4,256,1792]{1,2,0:T(8,128)} %get-tuple-element.21, f32[4,256]{1,0:T(4,128)S(1)} %get-tuple-element.20), kind=kOutput, calls=%fused_computation.33 | convolution fusion | flops 482609920 | bytes 15863808 | tf_op jit(solution)/shard_map/htk,thd->kd/dot_general | solution.py:55
  109.5 1.3 fusion.29
  110.8 1.3 collective-permute-start.6
  112.1 5.1 %collective-permute-start.7 = (f32[256,256]{0,1:T(8,128)S(1)}, f32[256,256]{0,1:T(8,128)S(1)}, u32[]{:S(2)}, u32[]{:S(2)}) collective-permute-start(f32[256,256]{0,1:T(8,128)S(1)} %get-tuple-element.13), channel_id=1, source_target_pairs={{0,2},{2,4},{4,6},{6,8},{8,10},{10,12},{12,14},{1,3},{3,5},{5,7},{... | collective-permute-start | bytes 786440 | tf_op jit(solution)/shard_map/ppermute | solution.py:15
  117.2 1.3 collective-permute-start.8
  118.5 5.0 %collective-permute-start.9 = (f32[256,256]{0,1:T(8,128)S(1)}, f32[256,256]{0,1:T(8,128)S(1)}, u32[]{:S(2)}, u32[]{:S(2)}) collective-permute-start(f32[256,256]{0,1:T(8,128)S(1)} %get-tuple-element.15), channel_id=1, source_target_pairs={{0,4},{2,6},{4,8},{6,10},{8,12},{10,14},{1,5},{3,7},{5,9},{7,11},{... | collective-permute-start | bytes 786440 | tf_op jit(solution)/shard_map/ppermute | solution.py:15
  123.5 6.3 %collective-permute-start.11 = (f32[256,256]{0,1:T(8,128)S(1)}, f32[256,256]{0,1:T(8,128)S(1)}, u32[]{:S(2)}, u32[]{:S(2)}) collective-permute-start(f32[256,256]{0,1:T(8,128)S(1)} %get-tuple-element.16), channel_id=1, source_target_pairs={{0,6},{2,8},{4,10},{6,12},{8,14},{1,7},{3,9},{5,11},{7,13},{9,15},... | collective-permute-start | bytes 786440 | tf_op jit(solution)/shard_map/ppermute | solution.py:15
  129.8 1.3 collective-permute-start.10
  131.1 4.6 %collective-permute-done.11 = f32[256,256]{0,1:T(8,128)S(1)} collective-permute-done((f32[256,256]{0,1:T(8,128)S(1)}, f32[256,256]{0,1:T(8,128)S(1)}, u32[]{:S(2)}, u32[]{:S(2)}) %collective-permute-start.11) | collective-permute-done | bytes 262176 | tf_op jit(solution)/shard_map/ppermute | solution.py:15
  135.7 3.2 %collective-permute-done.10 = f32[256,256]{0,1:T(8,128)S(1)} collective-permute-done((f32[256,256]{0,1:T(8,128)S(1)}, f32[256,256]{0,1:T(8,128)S(1)}, u32[]{:S(2)}, u32[]{:S(2)}) %collective-permute-start.10) | collective-permute-done | bytes 262176 | tf_op jit(solution)/shard_map/ppermute | solution.py:15
  139.0 1.0 fusion.28
  140.0 4.3 %all-reduce.3 = bf16[256,256]{0,1:T(8,128)(2,1)S(1)} all-reduce(f32[256,256]{0,1:T(8,128)S(1)} %fusion.28), channel_id=1, replica_groups=mesh['groups'=2,'dp'=8,'fsdp'=2] {'fsdp'}, use_global_device_ids=true, to_apply=%region_8.9 | all-reduce | flops 65536 | bytes 393216 | tf_op jit(solution)/shard_map/psum | solution.py:105
  144.3 1.8 fusion.33
  146.2 11.9 %fusion.18 = bf16[128,4,256]{2,0,1:T(8,128)(2,1)S(1)} fusion(bf16[1792,128,1]{1,0,2:T(8,128)(2,1)} %bitcast.90, f32[1792,256,4]{1,0,2:T(8,128)} %fusion.45, f32[4,256,1792]{1,2,0:T(8,128)} %get-tuple-element.21, f32[4,256]{1,0:T(4,128)S(1)} %get-tuple-element.20), kind=kOutput, calls=%fused_computation.35 | convolution fusion | flops 482740992 | bytes 15405056 | tf_op jit(solution)/shard_map/htk,kd->thd/dot_general | solution.py:52
  159.6 2.0 convolution_convert_fusion
  161.7 55.7 %reduce-scatter.2.cloned.1.call-done = f32[16,4096]{1,0:T(8,128)} async-done(((f32[128,4096]{1,0:T(8,128)}), f32[16,4096]{1,0:T(8,128)}) %reduce-scatter.2.cloned.1.call-update) | async-done | bytes 262160 | tf_op jit(solution)/shard_map/reduce_scatter | solution.py:111
  (39 shorter events, 7.0 us)
Async XLA Ops:
  7.2 45.9 %copy-start = (bf16[256,4096]{1,0:T(8,128)(2,1)S(1)}, bf16[256,4096]{1,0:T(8,128)(2,1)}, u32[]{:S(2)}) copy-start(bf16[256,4096]{1,0:T(8,128)(2,1)} %param.7) | copy-start | bytes 6291460
  7.2 45.8 %all-gather.2.cloned.1.call-start = ((), (), s32[]{:S(2)}) async-start(), calls=%async_computation.1 | async-start | bytes 1179648 | tf_op jit(solution)/shard_map/all_gather | solution.py:70
  7.9 209.5 %reduce-scatter.2.cloned.1.call-start = ((), (), s32[]{:S(2)}) async-start(), calls=%async_computation.2 | async-start | bytes 2359296 | tf_op jit(solution)/shard_map/reduce_scatter | solution.py:111
  59.7 15.3 %collective-permute-start = (bf16[256,256]{1,0:T(8,128)(2,1)S(1)}, bf16[256,256]{1,0:T(8,128)(2,1)}, u32[]{:S(2)}, u32[]{:S(2)}) collective-permute-start(bf16[256,256]{1,0:T(8,128)(2,1)S(1)} %pad_maximum_fusion.1), channel_id=1, source_target_pairs={{0,6},{2,8},{4,10},{6,12},{8,14},{1,7},{3,9},{5,11},{7,13},{9,15},... | collective-permute-start | bytes 393224 | tf_op jit(solution)/shard_map/ppermute | solution.py:15
  66.5 17.1 %collective-permute-start.4 = (bf16[256,256]{1,0:T(8,128)(2,1)S(1)}, bf16[256,256]{1,0:T(8,128)(2,1)S(1)}, u32[]{:S(2)}, u32[]{:S(2)}) collective-permute-start(bf16[256,256]{1,0:T(8,128)(2,1)S(1)} %pad_maximum_fusion.1), channel_id=1, source_target_pairs={{4,0},{6,2},{8,4},{10,6},{12,8},{14,10},{5,1},{7,3},{9,5},{11,7},{... | collective-permute-start | bytes 393224 | tf_op jit(solution)/shard_map/ppermute | solution.py:15
  67.8 15.8 %collective-permute-start.3 = (bf16[256,256]{1,0:T(8,128)(2,1)S(1)}, bf16[256,256]{1,0:T(8,128)(2,1)S(1)}, u32[]{:S(2)}, u32[]{:S(2)}) collective-permute-start(bf16[256,256]{1,0:T(8,128)(2,1)S(1)} %pad_maximum_fusion.1), channel_id=1, source_target_pairs={{2,0},{4,2},{6,4},{8,6},{10,8},{12,10},{14,12},{3,1},{5,3},{7,5},{... | collective-permute-start | bytes 393224 | tf_op jit(solution)/shard_map/ppermute | solution.py:15
  69.1 14.5 %collective-permute-start.5 = (bf16[256,256]{1,0:T(8,128)(2,1)S(1)}, bf16[256,256]{1,0:T(8,128)(2,1)S(1)}, u32[]{:S(2)}, u32[]{:S(2)}) collective-permute-start(bf16[256,256]{1,0:T(8,128)(2,1)S(1)} %pad_maximum_fusion.1), channel_id=1, source_target_pairs={{6,0},{8,2},{10,4},{12,6},{14,8},{7,1},{9,3},{11,5},{13,7},{15,9},... | collective-permute-start | bytes 393224 | tf_op jit(solution)/shard_map/ppermute | solution.py:15
  70.4 12.3 %collective-permute-start.2 = (bf16[256,256]{1,0:T(8,128)(2,1)S(1)}, bf16[256,256]{1,0:T(8,128)(2,1)S(1)}, u32[]{:S(2)}, u32[]{:S(2)}) collective-permute-start(bf16[256,256]{1,0:T(8,128)(2,1)S(1)} %pad_maximum_fusion.1), channel_id=1, source_target_pairs={{0,2},{2,4},{4,6},{6,8},{8,10},{10,12},{12,14},{1,3},{3,5},{5,7},{... | collective-permute-start | bytes 393224 | tf_op jit(solution)/shard_map/ppermute | solution.py:15
  75.0 7.7 %collective-permute-start.1 = (bf16[256,256]{1,0:T(8,128)(2,1)S(1)}, bf16[256,256]{1,0:T(8,128)(2,1)S(1)}, u32[]{:S(2)}, u32[]{:S(2)}) collective-permute-start(bf16[256,256]{1,0:T(8,128)(2,1)S(1)} %pad_maximum_fusion.1), channel_id=1, source_target_pairs={{0,4},{2,6},{4,8},{6,10},{8,12},{10,14},{1,5},{3,7},{5,9},{7,11},{... | collective-permute-start | bytes 393224 | tf_op jit(solution)/shard_map/ppermute | solution.py:15
  83.8 9.7 %copy-start.2 = (bf16[7,256,128]{2,1,0:T(8,128)(2,1)}, bf16[7,256,128]{2,1,0:T(8,128)(2,1)S(1)}, u32[]{:S(2)}) copy-start(bf16[7,256,128]{2,1,0:T(8,128)(2,1)S(1)} %get-tuple-element.19) | copy-start | bytes 1376260
  110.8 18.9 %collective-permute-start.6 = (f32[256,256]{0,1:T(8,128)S(1)}, f32[256,256]{0,1:T(8,128)S(1)}, u32[]{:S(2)}, u32[]{:S(2)}) collective-permute-start(f32[256,256]{0,1:T(8,128)S(1)} %get-tuple-element.12), channel_id=1, source_target_pairs={{2,0},{4,2},{6,4},{8,6},{10,8},{12,10},{14,12},{3,1},{5,3},{7,5},{... | collective-permute-start | bytes 786440 | tf_op jit(solution)/shard_map/ppermute | solution.py:15
  112.1 19.0 %collective-permute-start.7 = (f32[256,256]{0,1:T(8,128)S(1)}, f32[256,256]{0,1:T(8,128)S(1)}, u32[]{:S(2)}, u32[]{:S(2)}) collective-permute-start(f32[256,256]{0,1:T(8,128)S(1)} %get-tuple-element.13), channel_id=1, source_target_pairs={{0,2},{2,4},{4,6},{6,8},{8,10},{10,12},{12,14},{1,3},{3,5},{5,7},{... | collective-permute-start | bytes 786440 | tf_op jit(solution)/shard_map/ppermute | solution.py:15
  117.2 13.9 %collective-permute-start.8 = (f32[256,256]{0,1:T(8,128)S(1)}, f32[256,256]{0,1:T(8,128)S(1)}, u32[]{:S(2)}, u32[]{:S(2)}) collective-permute-start(f32[256,256]{0,1:T(8,128)S(1)} %get-tuple-element.14), channel_id=1, source_target_pairs={{4,0},{6,2},{8,4},{10,6},{12,8},{14,10},{5,1},{7,3},{9,5},{11,7},{... | collective-permute-start | bytes 786440 | tf_op jit(solution)/shard_map/ppermute | solution.py:15
  118.5 12.6 %collective-permute-start.9 = (f32[256,256]{0,1:T(8,128)S(1)}, f32[256,256]{0,1:T(8,128)S(1)}, u32[]{:S(2)}, u32[]{:S(2)}) collective-permute-start(f32[256,256]{0,1:T(8,128)S(1)} %get-tuple-element.15), channel_id=1, source_target_pairs={{0,4},{2,6},{4,8},{6,10},{8,12},{10,14},{1,5},{3,7},{5,9},{7,11},{... | collective-permute-start | bytes 786440 | tf_op jit(solution)/shard_map/ppermute | solution.py:15
  123.5 12.2 %collective-permute-start.11 = (f32[256,256]{0,1:T(8,128)S(1)}, f32[256,256]{0,1:T(8,128)S(1)}, u32[]{:S(2)}, u32[]{:S(2)}) collective-permute-start(f32[256,256]{0,1:T(8,128)S(1)} %get-tuple-element.16), channel_id=1, source_target_pairs={{0,6},{2,8},{4,10},{6,12},{8,14},{1,7},{3,9},{5,11},{7,13},{9,15},... | collective-permute-start | bytes 786440 | tf_op jit(solution)/shard_map/ppermute | solution.py:15
  129.8 9.2 %collective-permute-start.10 = (f32[256,256]{0,1:T(8,128)S(1)}, f32[256,256]{0,1:T(8,128)S(1)}, u32[]{:S(2)}, u32[]{:S(2)}) collective-permute-start(f32[256,256]{0,1:T(8,128)S(1)} %get-tuple-element.17), channel_id=1, source_target_pairs={{6,0},{8,2},{10,4},{12,6},{14,8},{7,1},{9,3},{11,5},{13,7},{15,9},... | collective-permute-start | bytes 786440 | tf_op jit(solution)/shard_map/ppermute | solution.py:15
  146.1 13.5 %copy-start.1 = (bf16[4096,128]{0,1:T(8,128)(2,1)S(1)}, bf16[4096,128]{0,1:T(8,128)(2,1)}, u32[]{:S(2)}) copy-start(bf16[4096,128]{0,1:T(8,128)(2,1)} %all-gather.2.cloned.1.call-done) | copy-start | bytes 3145732
Sparse Core Ops, SparseCore 0:
  10.1 42.8 all-gather.1
  146.3 71.0 reduce-scatter.1
where the time goes:
time: 225 us; the launch traced here: 224 us
  waiting for transfers between devices  109 us (48%)
  matrix products  43.3 us (19%)
  starting transfers between devices  37 us (16%)
  between operations  14.4 us (6%)
  blocking collectives  8.2 us (4%)
  other arithmetic  7.43 us (3%)
  local copies, waits for them, and re-layouts  4.89 us (2%)
    reduce_scatter x1, waiting for transfers between devices, body(): lax.psum_scatter(lax.dot_general(grad_value, layer_input, (((0,), (0,)),...  55.7 us
    all_gather x1, waiting for transfers between devices, body(): full_weight = lax.all_gather(w_value, 'dp', axis=1, tiled=True)  43.3 us
    ppermute x12, starting transfers between devices, passed_along(): lax.ppermute(value, axis, [(source, source + steps) for source in range(l...  36.9 us
    dot_general x1, matrix products, grad_block(): jnp.einsum('htk,kd->thd', grad_scores, key_block, preferred_element_type=...  11.9 us
    dot_general x1, matrix products, grad_block(): jnp.einsum('htk,thd->kd', grad_scores, query_rows, preferred_element_type...  11.6 us
    ppermute x12, waiting for transfers between devices, passed_along(): lax.ppermute(value, axis, [(source, source + steps) for source in range(l...  9.44 us
    sub x1, matrix products, body(): expos = jnp.exp(scores - peak)  5.59 us
  transfers between devices with their start and end apart: 14, of which 5 were waited for; matrix products, arithmetic and copies ran while one was open for 10% of the time, Pallas kernels for 0%

commit v1 on v0

v1 whole, which is shorter than its diff:
```python
import math

import jax
import jax.numpy as jnp
from jax import lax
from jax.experimental import pallas as pl
from jax.experimental.pallas import tpu as pltpu
from jax.sharding import PartitionSpec as P

SPAN = 3
NEGATIVE = -1e30
CHUNK = 256
ROWS = 128
BOTH = ("dp", "fsdp")
F32 = jnp.float32
BF16 = jnp.bfloat16
VMEM = pl.BlockSpec(memory_space=pltpu.VMEM)
SMEM = pl.BlockSpec(memory_space=pltpu.SMEM)


def core_swap(value):
    return lax.ppermute(value, "fsdp", [(0, 1), (1, 0)])


def dp_swap(value, mask):
    count = lax.axis_size("dp")
    return lax.ppermute(value, "dp", [(i, i ^ mask) for i in range(count)])


def fan_out(value, distance):
    count = lax.axis_size("dp")
    pairs = [(2 * i, 2 * (i + distance)) for i in range(count - distance)]
    pairs += [(2 * i + 1, 2 * (i - distance) + 1) for i in range(distance, count)]
    return lax.ppermute(value, BOTH, pairs)


def fan_back(value, distance):
    count = lax.axis_size("dp")
    pairs = [(2 * i, 2 * (i - distance)) for i in range(distance, count)]
    pairs += [(2 * i + 1, 2 * (i + distance) + 1) for i in range(count - distance)]
    return lax.ppermute(value, BOTH, pairs)


def chunk_range(first, window_first, lengths_ref, spans_ref, rows_too):
    last = first + ROWS - 1
    zero = jnp.int32(0)
    if rows_too:
        position = first + lax.broadcasted_iota(jnp.int32, (ROWS, 128), 0)
        low, high = jnp.zeros((ROWS, 128), jnp.int32), jnp.zeros((ROWS, 128), jnp.int32)
    else:
        position, low, high = zero, zero, zero

    def step(doc, carry):
        start, least, most, low, high = carry
        length = lengths_ref[doc]
        end = start + length
        bound = start + jnp.minimum(spans_ref[doc], length)
        least = jnp.where((start <= first) & (first < end), start, least)
        most = jnp.where((start <= last) & (last < end), jnp.maximum(last + 1, bound), most)
        if rows_too:
            inside = (position >= start) & (position < end)
            low = jnp.where(inside, start, low)
            high = jnp.where(inside, jnp.maximum(position + 1, bound), high)
        return (end, least, most, low, high)

    carry = (zero, zero, zero, low, high)
    count = lengths_ref.shape[0]
    if count <= 8:
        for doc in range(count):
            carry = step(doc, carry)
    else:
        carry = lax.fori_loop(0, count, step, carry)
    _, least, most, low, high = carry
    chunk_low = lax.div(least - window_first, CHUNK)
    chunk_high = lax.div(most - window_first + CHUNK - 1, CHUNK)
    return chunk_low, chunk_high, low, high


def place_window(core, window_ref, own_ref, mine, other):
    rows = own_ref.shape[0]
    window_ref[SPAN * rows : (SPAN + 1) * rows, :] = own_ref[...]

    def fill(behind, ahead):
        for k in range(1, SPAN + 1):
            window_ref[(SPAN - k) * rows : (SPAN - k + 1) * rows, :] = behind[k - 1][...]
            window_ref[(SPAN + k) * rows : (SPAN + k + 1) * rows, :] = ahead[k - 1][...]

    @pl.when(core == 0)
    def _():
        fill(mine, other)

    @pl.when(core == 1)
    def _():
        fill(other, mine)


def give_out(core, total_ref, own_ref, mine_ref, give_ref, factor):
    rows = own_ref.shape[0]

    def block(index):
        return total_ref[index * rows : (index + 1) * rows, :] * factor

    own_ref[...] = block(SPAN)
    for k in range(1, SPAN + 1):

        @pl.when(core == 0)
        def _():
            mine_ref[k - 1] = block(SPAN - k)
            give_ref[k - 1] = block(SPAN + k)

        @pl.when(core == 1)
        def _():
            mine_ref[k - 1] = block(SPAN + k)
            give_ref[k - 1] = block(SPAN - k)


def stack_heads(ref, first, out_ref):
    for h in range(ref.shape[1] // 128):
        out_ref[h * ROWS : (h + 1) * ROWS, :] = ref[first : first + ROWS, h * 128 : (h + 1) * 128]


def nt_dot(a, b):
    return lax.dot_general(a, b, (((1,), (1,)), ((), ())), preferred_element_type=F32)


def tn_dot(a, b):
    return lax.dot_general(a, b, (((0,), (0,)), ((), ())), preferred_element_type=F32)


def weights_kernel(
    place_ref, lengths_ref, spans_ref, q_ref, grad_ref, key_ref, r1, r2, r3, s1, s2, s3,
    probs_ref, scaled_ref, inverse_ref, window_ref, own_ref, mine_ref, give_ref,
    score_ref, peak_ref, sum_ref, stack_ref, total_ref,
):
    rows = key_ref.shape[0]
    heads = q_ref.shape[1] // 128
    me, core = place_ref[0], place_ref[1]
    place_window(core, window_ref, key_ref, (r1, r2, r3), (s1, s2, s3))
    total_ref[...] = jnp.zeros_like(total_ref)
    window_first = (me - SPAN) * rows
    lane = lax.broadcasted_iota(jnp.int32, (ROWS, 128), 1)
    power = math.log2(math.e) / math.sqrt(128.0)
    for part in range(rows // ROWS):
        stack_heads(q_ref, part * ROWS, stack_ref)
        chunk_low, chunk_high, low, high = chunk_range(
            me * rows + part * ROWS, window_first, lengths_ref, spans_ref, True
        )
        low = low - lane
        high = high - lane
        peak_ref[...] = jnp.full_like(peak_ref, NEGATIVE)
        sum_ref[...] = jnp.zeros_like(sum_ref)

        def score_step(chunk, _):
            keys = window_ref[pl.ds(pl.multiple_of(chunk * CHUNK, CHUNK), CHUNK), :]
            scores = nt_dot(stack_ref[...], keys).reshape(heads, ROWS, CHUNK)
            peak = peak_ref[...]
            for half in range(CHUNK // 128):
                base = window_first + chunk * CHUNK + half * 128
                seen = (low <= base) & (base < high)
                masked = jnp.where(seen[None], scores[:, :, half * 128 : (half + 1) * 128], NEGATIVE)
                score_ref[chunk, :, :, half * 128 : (half + 1) * 128] = masked
                peak = jnp.maximum(peak, masked)
            peak_ref[...] = peak
            return 0

        lax.fori_loop(chunk_low, chunk_high, score_step, 0)
        peak = jnp.max(peak_ref[...], axis=2, keepdims=True)
        peak_ref[...] = jnp.broadcast_to(peak, peak_ref.shape)

        def exp_step(chunk, _):
            total = sum_ref[...]
            peak = peak_ref[...]
            for half in range(CHUNK // 128):
                cut = slice(half * 128, (half + 1) * 128)
                probs = jnp.exp2((score_ref[chunk, :, :, cut] - peak) * power)
                total = total + probs
                probs_ref[part, chunk, :, cut] = probs.reshape(heads * ROWS, 128).astype(BF16)
            sum_ref[...] = total
            return 0

        lax.fori_loop(chunk_low, chunk_high, exp_step, 0)
        inverse = 1.0 / jnp.sum(sum_ref[...], axis=2, keepdims=True)
        inverse_ref[part] = jnp.broadcast_to(inverse, sum_ref.shape).reshape(heads * ROWS, 128)
        for h in range(heads):
            grads = grad_ref[part * ROWS : (part + 1) * ROWS, h * 128 : (h + 1) * 128]
            scaled_ref[part, h * ROWS : (h + 1) * ROWS, :] = (
                grads.astype(F32) * inverse[h]
            ).astype(BF16)

        def value_step(chunk, _):
            at = pl.ds(pl.multiple_of(chunk * CHUNK, CHUNK), CHUNK)
            total_ref[at, :] += tn_dot(probs_ref[part, chunk], scaled_ref[part])
            return 0

        lax.fori_loop(chunk_low, chunk_high, value_step, 0)
    give_out(core, total_ref, own_ref, mine_ref, give_ref, 1.0)


def scores_kernel(
    place_ref, lengths_ref, spans_ref, q_ref, scaled_ref, inverse_ref, probs_ref, keys_ref, value_ref,
    r1, r2, r3, s1, s2, s3,
    grad_q_ref, own_ref, mine_ref, give_ref,
    values_ref, product_ref, delta_ref, stack_ref, query_ref, total_ref,
):
    rows = value_ref.shape[0]
    heads = q_ref.shape[1] // 128
    me, core = place_ref[0], place_ref[1]
    place_window(core, values_ref, value_ref, (r1, r2, r3), (s1, s2, s3))
    total_ref[...] = jnp.zeros_like(total_ref)
    window_first = (me - SPAN) * rows
    scaling = 1.0 / math.sqrt(128.0)
    for part in range(rows // ROWS):
        stack_heads(q_ref, part * ROWS, stack_ref)
        chunk_low, chunk_high, _, _ = chunk_range(
            me * rows + part * ROWS, window_first, lengths_ref, spans_ref, False
        )
        delta_ref[...] = jnp.zeros_like(delta_ref)
        query_ref[...] = jnp.zeros_like(query_ref)

        def delta_step(chunk, _):
            at = pl.ds(pl.multiple_of(chunk * CHUNK, CHUNK), CHUNK)
            product = nt_dot(scaled_ref[part], values_ref[at, :])
            product_ref[chunk] = product
            terms = product * probs_ref[part, chunk].astype(F32)
            delta = delta_ref[...]
            for half in range(CHUNK // 128):
                delta = delta + terms[:, half * 128 : (half + 1) * 128]
            delta_ref[...] = delta
            return 0

        lax.fori_loop(chunk_low, chunk_high, delta_step, 0)
        delta = jnp.sum(delta_ref[...], axis=1, keepdims=True)
        delta_ref[...] = delta * inverse_ref[part]

        def grad_step(chunk, _):
            at = pl.ds(pl.multiple_of(chunk * CHUNK, CHUNK), CHUNK)
            probs = probs_ref[part, chunk].astype(F32)
            delta = delta_ref[...]
            product = product_ref[chunk]
            grad = jnp.concatenate(
                [
                    (probs[:, cut] * (product[:, cut] - delta)).astype(BF16)
                    for cut in (slice(i, i + 128) for i in range(0, CHUNK, 128))
                ],
                axis=1,
            )
            query_ref[...] += jnp.dot(grad, keys_ref[at, :], preferred_element_type=F32)
            total_ref[at, :] += tn_dot(grad, stack_ref[...])
            return 0

        lax.fori_loop(chunk_low, chunk_high, grad_step, 0)
        for h in range(heads):
            grad_q_ref[part * ROWS : (part + 1) * ROWS, h * 128 : (h + 1) * 128] = (
                query_ref[h * ROWS : (h + 1) * ROWS, :] * scaling
            ).astype(BF16)
    give_out(core, total_ref, own_ref, mine_ref, give_ref, scaling)


def value_kernel(place_ref, x_ref, own_ref, z1, z2, z3, other_ref, part_ref, weight_ref):
    me = place_ref[0]
    width = own_ref.shape[0]
    for k, block in enumerate((own_ref, z1, z2, z3)):
        owner = me ^ (2 * k)
        weight_ref[pl.ds(pl.multiple_of(owner * width, width), width), :] = block[...]
        there = owner ^ 1
        weight_ref[pl.ds(pl.multiple_of(there * width, width), width), :] = other_ref[k]
    part_ref[...] = nt_dot(x_ref[...], weight_ref[...])


def weight_grad_kernel(place_ref, a_ref, b_ref, x_ref, grad_ref, keep_ref, send_ref):
    me = place_ref[0]
    grad = (a_ref[...] + b_ref[...]).astype(BF16)
    grad_ref[...] = grad
    depth = x_ref.shape[1]
    width = keep_ref.shape[1]
    step = 512
    for at in range(0, depth, step):
        out = tn_dot(grad, x_ref[:, at : at + step])
        for owner in range(2 * keep_ref.shape[0]):
            rows = out[owner * width : (owner + 1) * width, :]

            @pl.when(lax.rem(me, 2) == owner % 2)
            def _():
                keep_ref[owner // 2, :, at : at + step] = rows

            @pl.when(lax.rem(me, 2) != owner % 2)
            def _():
                send_ref[owner // 2, :, at : at + step] = rows.astype(BF16)


def pair_sum_kernel(place_ref, keep_ref, came_ref, own_ref, z1, z2, z3):
    row = lax.div(place_ref[0], 2)
    own_ref[...] = keep_ref[row] + came_ref[row].astype(F32)
    for k, out in enumerate((z1, z2, z3)):
        there = row ^ (k + 1)
        out[...] = (keep_ref[there] + came_ref[there].astype(F32)).astype(BF16)


def call(kernel, outs, scratch, limit_mib, flops, moved, *args):
    smem = 3 if kernel in (weights_kernel, scores_kernel) else 1
    return pl.pallas_call(
        kernel,
        in_specs=[SMEM] * smem + [VMEM] * (len(args) - smem),
        out_specs=[VMEM] * len(outs),
        out_shape=[jax.ShapeDtypeStruct(shape, kind) for shape, kind in outs],
        scratch_shapes=scratch,
        compiler_params=pltpu.CompilerParams(vmem_limit_bytes=limit_mib << 20),
        cost_estimate=pl.CostEstimate(flops=flops, bytes_accessed=moved, transcendentals=0),
    )(*args)


def returned(own, mine, give):
    got = core_swap(give)
    for k in range(1, SPAN + 1):
        own = own + fan_back((mine[k - 1] + got[k - 1]).astype(BF16), k).astype(F32)
    return own


def body(layer_input, w_value, queries, keys, grad_out, doc_lengths, prefix_spans):
    rows, depth = layer_input.shape
    head = keys.shape[1]
    heads = queries.shape[1] // head
    dp = lax.axis_size("dp")
    window = (2 * SPAN + 1) * rows
    chunks = window // CHUNK
    parts = rows // ROWS
    stack = heads * ROWS
    place = jnp.stack([lax.axis_index("dp"), lax.axis_index("fsdp")]).astype(jnp.int32)
    weight = w_value.T
    width = weight.shape[0]
    direct = dp == 8

    mine = [fan_out(keys, k) for k in range(1, SPAN + 1)]
    other = [core_swap(block) for block in mine]

    if direct:
        columns = [dp_swap(weight, 2 * k) for k in range(1, 4)]
        across = dp_swap(jnp.stack([weight] + columns), 1)

    probs, scaled, inverse, key_window, own, mine_v, give_v = call(
        weights_kernel,
        [
            ((parts, chunks, stack, CHUNK), BF16),
            ((parts, stack, head), BF16),
            ((parts, stack, 128), F32),
            ((window, head), BF16),
            ((rows, head), F32),
            ((SPAN, rows, head), F32),
            ((SPAN, rows, head), F32),
        ],
        [
            pltpu.VMEM((chunks, heads, ROWS, CHUNK), F32),
            pltpu.VMEM((heads, ROWS, 128), F32),
            pltpu.VMEM((heads, ROWS, 128), F32),
            pltpu.VMEM((stack, head), BF16),
            pltpu.VMEM((window, head), F32),
        ],
        24, 1 << 30, 6 << 20,
        place, doc_lengths, prefix_spans, queries, grad_out, keys, *mine, *other,
    )
    half_v = returned(own, mine_v, give_v)
    other_v = core_swap(half_v)

    if direct:
        value_part, full_weight = call(
            value_kernel,
            [((rows, head), F32), ((head, depth), BF16)],
            [], 16, 1 << 28, 4 << 20,
            place, layer_input, weight, *columns, across,
        )
    else:
        full_weight = lax.all_gather(weight, "dp", axis=0, tiled=True)
        value_part = nt_dot(layer_input, full_weight)
    value = (value_part + core_swap(value_part)).astype(BF16)
    mine_x = [fan_out(value, k) for k in range(1, SPAN + 1)]
    other_x = [core_swap(block) for block in mine_x]

    if direct:
        grad_value, keep, send = call(
            weight_grad_kernel,
            [((rows, head), BF16), ((4, width, depth), F32), ((4, width, depth), BF16)],
            [], 16, 1 << 28, 4 << 20,
            place, half_v, other_v, layer_input,
        )
        came = dp_swap(send, 1)
        total, *sends = call(
            pair_sum_kernel,
            [((width, depth), F32)] + [((width, depth), BF16)] * 3,
            [], 16, 1 << 20, 2 << 20,
            place, keep, came,
        )
        for k in range(1, 4):
            total = total + dp_swap(sends[k - 1], 2 * k).astype(F32)
        grad_weight = total.T
    else:
        grad_value = (half_v + other_v).astype(BF16)
        grad_weight = lax.psum_scatter(
            tn_dot(grad_value, layer_input), "dp", scatter_dimension=0, tiled=True
        ).T
    grad_input = jnp.dot(grad_value, full_weight, preferred_element_type=F32).astype(BF16)

    grad_queries, own, mine_k, give_k = call(
        scores_kernel,
        [
            ((rows, heads * head), BF16),
            ((rows, head), F32),
            ((SPAN, rows, head), F32),
            ((SPAN, rows, head), F32),
        ],
        [
            pltpu.VMEM((window, head), BF16),
            pltpu.VMEM((chunks, stack, CHUNK), F32),
            pltpu.VMEM((stack, 128), F32),
            pltpu.VMEM((stack, head), BF16),
            pltpu.VMEM((stack, head), F32),
            pltpu.VMEM((window, head), F32),
        ],
        24, 1 << 30, 6 << 20,
        place, doc_lengths, prefix_spans, queries, scaled, inverse, probs, key_window, value,
        *mine_x, *other_x,
    )
    half_k = returned(own, mine_k, give_k)
    grad_keys = (half_k + core_swap(half_k)).astype(BF16)
    return (grad_input, grad_queries, grad_keys, grad_weight)


def solution(mesh):
    in_specs = (
        P(("groups", "dp"), "fsdp"),
        P("fsdp", "dp"),
        P(("groups", "dp"), "fsdp"),
        P(("groups", "dp"), None),
        P(("groups", "dp"), "fsdp"),
        P("groups"),
        P("groups"),
    )
    out_specs = (
        P(("groups", "dp"), "fsdp"),
        P(("groups", "dp"), "fsdp"),
        P(("groups", "dp"), None),
        P(("groups", "fsdp"), "dp"),
    )
    return jax.shard_map(body, mesh=mesh, in_specs=in_specs, out_specs=out_specs, check_vma=False)
```

time: 225 us -> 105 us (0.47)
  waiting for transfers between devices: 109 us -> 33.2 us
  matrix products: 43.3 us -> 2.02 us
  starting transfers between devices: 37 us -> 52.9 us
  between operations: 14.4 us -> 0.99 us
  Pallas kernels: 0 us -> 10.2 us
  blocking collectives: 8.2 us -> 0 us
  other arithmetic: 7.43 us -> 2.68 us
  local copies, waits for them, and re-layouts: 4.89 us -> 2.52 us
    reduce_scatter x1 -> x0, waiting for transfers between devices: 55.7 us -> none  [body(): lax.psum_scatter(lax.dot_general(grad_value, layer_input, (((0,), (0,)),...]
    all_gather x1 -> x0, waiting for transfers between devices: 43.3 us -> none  [body(): full_weight = lax.all_gather(w_value, 'dp', axis=1, tiled=True)]
    dot_general x7 -> x1, matrix products: 37.7 us -> 2.02 us  [body(): jnp.dot(grad_value, full_weight, preferred_element_type=F32).astype(BF16)]
    ppermute x12 -> x31, waiting for transfers between devices: 9.44 us -> 33.2 us  [the longest x8 28.1 us: dp_swap(): return lax.ppermute(value, 'dp', [(i, i ^ mask) for i in range(count)])]
    ppermute x12 -> x31, starting transfers between devices: 36.9 us -> 52.9 us  [the longest x6 21.8 us: fan_out(): return lax.ppermute(value, BOTH, pairs)]
    pallas_call x0 -> x5, Pallas kernels: none -> 10.2 us  [call(): pl.pallas_call(kernel, in_specs=[SMEM] * smem + [VMEM] * (len(args) - sme...]
    psum x2 -> x0, blocking collectives: 8.2 us -> none  [the longest x1 4.35 us: body(): summed = lax.psum(gathered, 'fsdp')]
    sub x1 -> x0, matrix products: 5.59 us -> none  [body(): expos = jnp.exp(scores - peak)]
  transfers between devices with their start and end apart: 14 -> 31, of which waited for: 5 -> 8; matrix products, arithmetic and copies ran while one was open for 10% -> 3% of each run, Pallas kernels for 0% -> 10%
where the time goes in v1:
time: 105 us; the launch traced here: 104 us
  starting transfers between devices  52.9 us (50%)
  waiting for transfers between devices  33.2 us (32%)
  Pallas kernels  10.2 us (10%)
  other arithmetic  2.68 us (3%)
  local copies, waits for them, and re-layouts  2.52 us (2%)
  matrix products  2.02 us (2%)
    ppermute x8, waiting for transfers between devices, dp_swap(): return lax.ppermute(value, 'dp', [(i, i ^ mask) for i in range(count)])  28.1 us
    ppermute x6, starting transfers between devices, fan_out(): return lax.ppermute(value, BOTH, pairs)  21.8 us
    ppermute x8, starting transfers between devices, dp_swap(): return lax.ppermute(value, 'dp', [(i, i ^ mask) for i in range(count)])  15 us
    pallas_call x5, Pallas kernels, call(): pl.pallas_call(kernel, in_specs=[SMEM] * smem + [VMEM] * (len(args) - sme...  10.2 us
    ppermute x11, starting transfers between devices, core_swap(): return lax.ppermute(value, 'fsdp', [(0, 1), (1, 0)])  8.4 us
    ppermute x6, starting transfers between devices, fan_back(): return lax.ppermute(value, BOTH, pairs)  7.75 us
    ppermute x6, waiting for transfers between devices, fan_out(): return lax.ppermute(value, BOTH, pairs)  3.67 us
    unnamed x16, local copies, waits for them, and re-layouts  2.52 us
  transfers between devices with their start and end apart: 31, of which 8 were waited for; matrix products, arithmetic and copies ran while one was open for 3% of the time, Pallas kernels for 10%

profile of v1, /device:TPU:0, one launch (start us, length us, event | category | flops | bytes accessed | tf_op | source)
XLA Modules:
  0.0 104.5 jit_solution(4219391443310241023)
XLA Ops:
  0.6 5.1 %collective-permute-start.13 = (bf16[16,4096]{1,0:T(8,128)(2,1)}, bf16[16,4096]{1,0:T(8,128)(2,1)S(1)}, u32[]{:S(2)}, u32[]{:S(2)}) collective-permute-start(bf16[16,4096]{1,0:T(8,128)(2,1)} %bitcast.24), channel_id=1, source_target_pairs={{0,12},{2,14},{4,8},{6,10},{8,4},{10,6},{12,0},{14,2},{1,13},{3,15... | collective-permute-start | bytes 393224 | tf_op jit(solution)/shard_map/ppermute | solution.py:27
  6.4 4.0 %collective-permute-done.13.z3 = bf16[16,4096]{1,0:T(8,128)(2,1)S(1)} collective-permute-done((bf16[16,4096]{1,0:T(8,128)(2,1)}, bf16[16,4096]{1,0:T(8,128)(2,1)S(1)}, u32[]{:S(2)}, u32[]{:S(2)}) %collective-permute-start.13) | collective-permute-done | bytes 131104 | tf_op jit(solution)/shard_map/ppermute | solution.py:27
  10.4 6.6 %collective-permute-done.12.z2 = bf16[16,4096]{1,0:T(8,128)(2,1)S(1)} collective-permute-done((bf16[16,4096]{1,0:T(8,128)(2,1)}, bf16[16,4096]{1,0:T(8,128)(2,1)S(1)}, u32[]{:S(2)}, u32[]{:S(2)}) %collective-permute-start.12) | collective-permute-done | bytes 131104 | tf_op jit(solution)/shard_map/ppermute | solution.py:27
  18.1 1.6 %collective-permute-start.14 = (bf16[4,16,4096]{2,1,0:T(8,128)(2,1)S(1)}, bf16[4,16,4096]{2,1,0:T(8,128)(2,1)S(1)}, u32[]{:S(2)}, u32[]{:S(2)}) collective-permute-start(bf16[4,16,4096]{2,1,0:T(8,128)(2,1)S(1)} %pad_maximum_fusion), channel_id=1, source_target_pairs={{0,2},{2,0},{4,6},{6,4},{8,10},{10,8},{12,14},{14,12},{1,3},{3,1},... | collective-permute-start | bytes 1572872 | tf_op jit(solution)/shard_map/ppermute | solution.py:27
  19.7 1.7 %collective-permute-start.1 = (bf16[256,128]{1,0:T(8,128)(2,1)}, bf16[256,128]{1,0:T(8,128)(2,1)S(1)}, u32[]{:S(2)}, u32[]{:S(2)}) collective-permute-start(bf16[256,128]{1,0:T(8,128)(2,1)} %key_ref.1), channel_id=1, source_target_pairs={{0,4},{2,6},{4,8},{6,10},{8,12},{10,14},{5,1},{7,3},{9,5},{11,7},{... | collective-permute-start | bytes 196616 | tf_op jit(solution)/shard_map/ppermute | solution.py:34
  21.4 2.4 %collective-permute-start = (bf16[256,128]{1,0:T(8,128)(2,1)}, bf16[256,128]{1,0:T(8,128)(2,1)S(1)}, u32[]{:S(2)}, u32[]{:S(2)}) collective-permute-start(bf16[256,128]{1,0:T(8,128)(2,1)} %key_ref.1), channel_id=1, source_target_pairs={{0,2},{2,4},{4,6},{6,8},{8,10},{10,12},{12,14},{3,1},{5,3},{7,5},{... | collective-permute-start | bytes 196616 | tf_op jit(solution)/shard_map/ppermute | solution.py:34
  23.8 6.1 %collective-permute-start.2 = (bf16[256,128]{1,0:T(8,128)(2,1)}, bf16[256,128]{1,0:T(8,128)(2,1)S(1)}, u32[]{:S(2)}, u32[]{:S(2)}) collective-permute-start(bf16[256,128]{1,0:T(8,128)(2,1)} %key_ref.1), channel_id=1, source_target_pairs={{0,6},{2,8},{4,10},{6,12},{8,14},{7,1},{9,3},{11,5},{13,7},{15,9},... | collective-permute-start | bytes 196616 | tf_op jit(solution)/shard_map/ppermute | solution.py:34
  30.0 2.4 %collective-permute-done.r1 = bf16[256,128]{1,0:T(8,128)(2,1)S(1)} collective-permute-done((bf16[256,128]{1,0:T(8,128)(2,1)}, bf16[256,128]{1,0:T(8,128)(2,1)S(1)}, u32[]{:S(2)}, u32[]{:S(2)}) %collective-permute-start) | collective-permute-done | bytes 65568 | tf_op jit(solution)/shard_map/ppermute | solution.py:34
  33.0 1.6 %copy-done = bf16[256,4096]{1,0:T(8,128)(2,1)S(1)} copy-done((bf16[256,4096]{1,0:T(8,128)(2,1)S(1)}, bf16[256,4096]{1,0:T(8,128)(2,1)}, u32[]{:S(2)}) %copy-start) | copy-done | bytes 2097176
  35.5 1.3 %shard_map.104 = (f32[256,128]{1,0:T(8,128)S(1)}, bf16[128,4096]{1,0:T(8,128)(2,1)S(1)}) custom-call(s32[2]{0:T(128)S(1)} %pad_add_fusion.place_ref, bf16[256,4096]{1,0:T(8,128)(2,1)S(1)} %copy-done, bf16[16,4096]{1,0:T(8,128)(2,1)S(1)} %bitcast.28, bf16[16,4096]{1,0:T(8,128)(2,1)S(1)} %collective-permute-done.11.z1, ...), custom_call_target="tpu_custom_call" | custom-call | flops 268435456 | bytes 4194304 | tf_op jit(solution)/shard_map/pallas_call | solution.py:301
  36.9 2.8 %shard_map.102 = (bf16[2,7,512,256]{3,2,1,0:T(8,128)(2,1)S(1)}, bf16[2,512,128]{2,1,0:T(8,128)(2,1)S(1)}, f32[2,512,128]{2,1,0:T(8,128)S(1)}, bf16[1792,128]{1,0...) custom-call(s32[2]{0:T(128)S(1)} %pad_add_fusion.place_ref, ...), custom_call_target="tpu_custom_call" | custom-call | flops 1073741824 | bytes 6291456 | tf_op jit(solution)/shard_map/pallas_call | solution.py:301
  40.3 5.5 %collective-permute-start.18 = (bf16[256,128]{1,0:T(8,128)(2,1)S(1)}, bf16[256,128]{1,0:T(8,128)(2,1)S(1)}, u32[]{:S(2)}, u32[]{:S(2)}) collective-permute-start(bf16[256,128]{1,0:T(8,128)(2,1)S(1)} %add_convert_fusion.1.value_ref), channel_id=1, source_target_pairs={{0,6},{2,8},{4,10},{6,12},{8,14},{7,1},{9,3},{11,5},{13,7},{15,9},... | collective-permute-start | bytes 196616 | tf_op jit(solution)/shard_map/ppermute | solution.py:34
  45.9 1.9 %collective-permute-start.17 = (bf16[256,128]{1,0:T(8,128)(2,1)S(1)}, bf16[256,128]{1,0:T(8,128)(2,1)S(1)}, u32[]{:S(2)}, u32[]{:S(2)}) collective-permute-start(bf16[256,128]{1,0:T(8,128)(2,1)S(1)} %add_convert_fusion.1.value_ref), channel_id=1, source_target_pairs={{0,4},{2,6},{4,8},{6,10},{8,12},{10,14},{5,1},{7,3},{9,5},{11,7},{... | collective-permute-start | bytes 196616 | tf_op jit(solution)/shard_map/ppermute | solution.py:34
  47.8 4.1 %collective-permute-start.16 = (bf16[256,128]{1,0:T(8,128)(2,1)S(1)}, bf16[256,128]{1,0:T(8,128)(2,1)S(1)}, u32[]{:S(2)}, u32[]{:S(2)}) collective-permute-start(bf16[256,128]{1,0:T(8,128)(2,1)S(1)} %add_convert_fusion.1.value_ref), channel_id=1, source_target_pairs={{0,2},{2,4},{4,6},{6,8},{8,10},{10,12},{12,14},{3,1},{5,3},{7,5},{... | collective-permute-start | bytes 196616 | tf_op jit(solution)/shard_map/ppermute | solution.py:34
  52.5 1.3 %collective-permute-done.16.r1 = bf16[256,128]{1,0:T(8,128)(2,1)S(1)} collective-permute-done((bf16[256,128]{1,0:T(8,128)(2,1)S(1)}, bf16[256,128]{1,0:T(8,128)(2,1)S(1)}, u32[]{:S(2)}, u32[]{:S(2)}) %collective-permute-start.16) | collective-permute-done | bytes 65568 | tf_op jit(solution)/shard_map/ppermute | solution.py:34
  53.8 1.3 %collective-permute-start.7 = (bf16[256,128]{1,0:T(8,128)(2,1)S(1)}, bf16[256,128]{1,0:T(8,128)(2,1)S(1)}, u32[]{:S(2)}, u32[]{:S(2)}) collective-permute-start(bf16[256,128]{1,0:T(8,128)(2,1)S(1)} %get-tuple-element.47), channel_id=1, source_target_pairs={{2,0},{4,2},{6,4},{8,6},{10,8},{12,10},{14,12},{1,3},{3,5},{5,7},{... | collective-permute-start | bytes 196616 | tf_op jit(solution)/shard_map/ppermute | solution.py:41
  55.1 1.3 %collective-permute-start.9 = (bf16[256,128]{1,0:T(8,128)(2,1)S(1)}, bf16[256,128]{1,0:T(8,128)(2,1)S(1)}, u32[]{:S(2)}, u32[]{:S(2)}) collective-permute-start(bf16[256,128]{1,0:T(8,128)(2,1)S(1)} %get-tuple-element.48), channel_id=1, source_target_pairs={{6,0},{8,2},{10,4},{12,6},{14,8},{1,7},{3,9},{5,11},{7,13},{9,15},... | collective-permute-start | bytes 196616 | tf_op jit(solution)/shard_map/ppermute | solution.py:41
  56.5 1.3 %collective-permute-start.8 = (bf16[256,128]{1,0:T(8,128)(2,1)S(1)}, bf16[256,128]{1,0:T(8,128)(2,1)S(1)}, u32[]{:S(2)}, u32[]{:S(2)}) collective-permute-start(bf16[256,128]{1,0:T(8,128)(2,1)S(1)} %get-tuple-element.49), channel_id=1, source_target_pairs={{4,0},{6,2},{8,4},{10,6},{12,8},{14,10},{1,5},{3,7},{5,9},{7,11},{... | collective-permute-start | bytes 196616 | tf_op jit(solution)/shard_map/ppermute | solution.py:41
  57.8 3.1 %shard_map.105 = (bf16[256,512]{1,0:T(8,128)(2,1)}, f32[256,128]{1,0:T(8,128)S(1)}, f32[3,256,128]{2,1,0:T(8,128)S(1)}, f32[3,256,128]{2,1,0:T(8,128)S(1)}) custom-call(s32[2]{0:T(128)S(1)} %pad_add_fusion.place_ref, s32[4]{0:T(128)S(1)} %copy-done.4, s32[4]{0:T(128)S(1)} %copy-done.5, bf16[256,512]{1,0:T(8,128)(2,1)S(1)} %copy-done.3, ...), custom_call_target="tpu_custom_call" | custom-call | flops 1073741824 | bytes 6291456 | tf_op jit(solution)/shard_map/pallas_call | solution.py:301
  60.8 6.5 %collective-permute-start.22 = (f32[3,256,128]{2,1,0:T(8,128)S(1)}, f32[3,256,128]{2,1,0:T(8,128)S(1)}, u32[]{:S(2)}, u32[]{:S(2)}) collective-permute-start(f32[3,256,128]{2,1,0:T(8,128)S(1)} %get-tuple-element.37), channel_id=1, source_target_pairs={{0,1},{1,0},{2,3},{3,2},{4,5},{5,4},{6,7},{7,6},{8,9},{9,8},{10,11... | collective-permute-start | bytes 1179656 | tf_op jit(solution)/shard_map/ppermute | solution.py:22
  67.5 1.4 %collective-permute-done.10.b_ref = f32[256,128]{1,0:T(8,128)S(1)} collective-permute-done((f32[256,128]{1,0:T(8,128)S(1)}, f32[256,128]{1,0:T(8,128)S(1)}, u32[]{:S(2)}, u32[]{:S(2)}) %collective-permute-start.10) | collective-permute-done | bytes 131104 | tf_op jit(solution)/shard_map/ppermute | solution.py:22
  68.9 2.4 %shard_map.103 = (bf16[256,128]{1,0:T(8,128)(2,1)S(1)}, f32[4,16,4096]{2,1,0:T(8,128)S(1)}, bf16[4,16,4096]{2,1,0:T(8,128)(2,1)S(1)}) custom-call(s32[2]{0:T(128)S(1)} %pad_add_fusion.place_ref, f32[256,128]{1,0:T(8,128)S(1)} %convert_add_fusion.1.a_ref, f32[256,128]{1,0:T(8,128)S(1)} %collective-permute-done.10.b_ref, bf16[256,4096]{1,0:T(8,128)(2,1)S(1)} %copy-done.1), custom_call_target="tpu_custom_call" | custom-call | flops 268435456 | bytes 4194304 | tf_op jit(solution)/shard_map/pallas_call | solution.py:301
  71.2 3.0 %collective-permute-start.27 = (bf16[4,16,4096]{2,1,0:T(8,128)(2,1)S(1)}, bf16[4,16,4096]{2,1,0:T(8,128)(2,1)S(1)}, u32[]{:S(2)}, u32[]{:S(2)}) collective-permute-start(bf16[4,16,4096]{2,1,0:T(8,128)(2,1)S(1)} %get-tuple-element.39), channel_id=1, source_target_pairs={{0,2},{2,0},{4,6},{6,4},{8,10},{10,8},{12,14},{14,12},{1,3},{3,1},... | collective-permute-start | bytes 1572872 | tf_op jit(solution)/shard_map/ppermute | solution.py:27
  74.3 1.3 %collective-permute-start.23 = (bf16[256,128]{1,0:T(8,128)(2,1)S(1)}, bf16[256,128]{1,0:T(8,128)(2,1)S(1)}, u32[]{:S(2)}, u32[]{:S(2)}) collective-permute-start(bf16[256,128]{1,0:T(8,128)(2,1)S(1)} %get-tuple-element.44), channel_id=1, source_target_pairs={{2,0},{4,2},{6,4},{8,6},{10,8},{12,10},{14,12},{1,3},{3,5},{5,7},{... | collective-permute-start | bytes 196616 | tf_op jit(solution)/shard_map/ppermute | solution.py:41
  75.6 1.3 %collective-permute-start.25 = (bf16[256,128]{1,0:T(8,128)(2,1)S(1)}, bf16[256,128]{1,0:T(8,128)(2,1)S(1)}, u32[]{:S(2)}, u32[]{:S(2)}) collective-permute-start(bf16[256,128]{1,0:T(8,128)(2,1)S(1)} %get-tuple-element.45), channel_id=1, source_target_pairs={{6,0},{8,2},{10,4},{12,6},{14,8},{1,7},{3,9},{5,11},{7,13},{9,15},... | collective-permute-start | bytes 196616 | tf_op jit(solution)/shard_map/ppermute | solution.py:41
  76.9 1.3 %collective-permute-start.24 = (bf16[256,128]{1,0:T(8,128)(2,1)S(1)}, bf16[256,128]{1,0:T(8,128)(2,1)S(1)}, u32[]{:S(2)}, u32[]{:S(2)}) collective-permute-start(bf16[256,128]{1,0:T(8,128)(2,1)S(1)} %get-tuple-element.46), channel_id=1, source_target_pairs={{4,0},{6,2},{8,4},{10,6},{12,8},{14,10},{1,5},{3,7},{5,9},{7,11},{... | collective-permute-start | bytes 196616 | tf_op jit(solution)/shard_map/ppermute | solution.py:41
  78.2 2.0 %convolution_convert_fusion = bf16[256,4096]{1,0:T(8,128)(2,1)} fusion(bf16[256,128]{1,0:T(8,128)(2,1)S(1)} %get-tuple-element.27, bf16[128,4096]{1,0:T(8,128)(2,1)S(1)} %get-tuple-element.28), kind=kOutput, calls=%fused_computation | convolution fusion | flops 269484032 | bytes 3211264 | tf_op jit(solution)/shard_map/dot_general | solution.py:400
  80.2 7.7 %collective-permute-done.27.came_ref = bf16[4,16,4096]{2,1,0:T(8,128)(2,1)S(1)} collective-permute-done((bf16[4,16,4096]{2,1,0:T(8,128)(2,1)S(1)}, bf16[4,16,4096]{2,1,0:T(8,128)(2,1)S(1)}, u32[]{:S(2)}, u32[]{:S(2)}) %collective-permute-start.27) | collective-permute-done | bytes 524320 | tf_op jit(solution)/shard_map/ppermute | solution.py:27
  88.6 1.1 %collective-permute-start.28 = (bf16[16,4096]{1,0:T(8,128)(2,1)S(1)}, bf16[16,4096]{1,0:T(8,128)(2,1)S(1)}, u32[]{:S(2)}, u32[]{:S(2)}) collective-permute-start(bf16[16,4096]{1,0:T(8,128)(2,1)S(1)} %get-tuple-element.41), channel_id=1, source_target_pairs={{0,4},{2,6},{4,0},{6,2},{8,12},{10,14},{12,8},{14,10},{1,5},{3,7},... | collective-permute-start | bytes 393224 | tf_op jit(solution)/shard_map/ppermute | solution.py:27
  89.7 3.4 %collective-permute-start.29 = (bf16[16,4096]{1,0:T(8,128)(2,1)S(1)}, bf16[16,4096]{1,0:T(8,128)(2,1)S(1)}, u32[]{:S(2)}, u32[]{:S(2)}) collective-permute-start(bf16[16,4096]{1,0:T(8,128)(2,1)S(1)} %get-tuple-element.42), channel_id=1, source_target_pairs={{0,8},{2,10},{4,12},{6,14},{8,0},{10,2},{12,4},{14,6},{1,9},{3,11}... | collective-permute-start | bytes 393224 | tf_op jit(solution)/shard_map/ppermute | solution.py:27
  93.3 1.9 %collective-permute-done.28 = bf16[16,4096]{1,0:T(8,128)(2,1)S(1)} collective-permute-done((bf16[16,4096]{1,0:T(8,128)(2,1)S(1)}, bf16[16,4096]{1,0:T(8,128)(2,1)S(1)}, u32[]{:S(2)}, u32[]{:S(2)}) %collective-permute-start.28) | collective-permute-done | bytes 131104 | tf_op jit(solution)/shard_map/ppermute | solution.py:27
  95.2 7.8 %collective-permute-done.29 = bf16[16,4096]{1,0:T(8,128)(2,1)S(1)} collective-permute-done((bf16[16,4096]{1,0:T(8,128)(2,1)S(1)}, bf16[16,4096]{1,0:T(8,128)(2,1)S(1)}, u32[]{:S(2)}, u32[]{:S(2)}) %collective-permute-start.29) | collective-permute-done | bytes 131104 | tf_op jit(solution)/shard_map/ppermute | solution.py:27
  (61 shorter events, 7.0 us)
Async XLA Ops:
  0.6 9.8 %collective-permute-start.13 = (bf16[16,4096]{1,0:T(8,128)(2,1)}, bf16[16,4096]{1,0:T(8,128)(2,1)S(1)}, u32[]{:S(2)}, u32[]{:S(2)}) collective-permute-start(bf16[16,4096]{1,0:T(8,128)(2,1)} %bitcast.24), channel_id=1, source_target_pairs={{0,12},{2,14},{4,8},{6,10},{8,4},{10,6},{12,0},{14,2},{1,13},{3,15... | collective-permute-start | bytes 393224 | tf_op jit(solution)/shard_map/ppermute | solution.py:27
  5.7 11.3 %collective-permute-start.12 = (bf16[16,4096]{1,0:T(8,128)(2,1)}, bf16[16,4096]{1,0:T(8,128)(2,1)S(1)}, u32[]{:S(2)}, u32[]{:S(2)}) collective-permute-start(bf16[16,4096]{1,0:T(8,128)(2,1)} %bitcast.25), channel_id=1, source_target_pairs={{0,8},{2,10},{4,12},{6,14},{8,0},{10,2},{12,4},{14,6},{1,9},{3,11}... | collective-permute-start | bytes 393224 | tf_op jit(solution)/shard_map/ppermute | solution.py:27
  5.7 11.3 %collective-permute-start.11 = (bf16[16,4096]{1,0:T(8,128)(2,1)}, bf16[16,4096]{1,0:T(8,128)(2,1)S(1)}, u32[]{:S(2)}, u32[]{:S(2)}) collective-permute-start(bf16[16,4096]{1,0:T(8,128)(2,1)} %bitcast.26), channel_id=1, source_target_pairs={{0,4},{2,6},{4,0},{6,2},{8,12},{10,14},{12,8},{14,10},{1,5},{3,7},... | collective-permute-start | bytes 393224 | tf_op jit(solution)/shard_map/ppermute | solution.py:27
  17.0 19.9 %copy-start.6 = (bf16[256,512]{1,0:T(8,128)(2,1)S(1)}, bf16[256,512]{1,0:T(8,128)(2,1)}, u32[]{:S(2)}) copy-start(bf16[256,512]{1,0:T(8,128)(2,1)} %grad_ref.1) | copy-start | bytes 786436
  18.1 14.9 %collective-permute-start.14 = (bf16[4,16,4096]{2,1,0:T(8,128)(2,1)S(1)}, bf16[4,16,4096]{2,1,0:T(8,128)(2,1)S(1)}, u32[]{:S(2)}, u32[]{:S(2)}) collective-permute-start(bf16[4,16,4096]{2,1,0:T(8,128)(2,1)S(1)} %pad_maximum_fusion), channel_id=1, source_target_pairs={{0,2},{2,0},{4,6},{6,4},{8,10},{10,8},{12,14},{14,12},{1,3},{3,1},... | collective-permute-start | bytes 1572872 | tf_op jit(solution)/shard_map/ppermute | solution.py:27
  19.7 10.3 %collective-permute-start.1 = (bf16[256,128]{1,0:T(8,128)(2,1)}, bf16[256,128]{1,0:T(8,128)(2,1)S(1)}, u32[]{:S(2)}, u32[]{:S(2)}) collective-permute-start(bf16[256,128]{1,0:T(8,128)(2,1)} %key_ref.1), channel_id=1, source_target_pairs={{0,4},{2,6},{4,8},{6,10},{8,12},{10,14},{5,1},{7,3},{9,5},{11,7},{... | collective-permute-start | bytes 196616 | tf_op jit(solution)/shard_map/ppermute | solution.py:34
  21.4 11.0 %collective-permute-start = (bf16[256,128]{1,0:T(8,128)(2,1)}, bf16[256,128]{1,0:T(8,128)(2,1)S(1)}, u32[]{:S(2)}, u32[]{:S(2)}) collective-permute-start(bf16[256,128]{1,0:T(8,128)(2,1)} %key_ref.1), channel_id=1, source_target_pairs={{0,2},{2,4},{4,6},{6,8},{8,10},{10,12},{12,14},{3,1},{5,3},{7,5},{... | collective-permute-start | bytes 196616 | tf_op jit(solution)/shard_map/ppermute | solution.py:34
  23.8 8.5 %collective-permute-start.2 = (bf16[256,128]{1,0:T(8,128)(2,1)}, bf16[256,128]{1,0:T(8,128)(2,1)S(1)}, u32[]{:S(2)}, u32[]{:S(2)}) collective-permute-start(bf16[256,128]{1,0:T(8,128)(2,1)} %key_ref.1), channel_id=1, source_target_pairs={{0,6},{2,8},{4,10},{6,12},{8,14},{7,1},{9,3},{11,5},{13,7},{15,9},... | collective-permute-start | bytes 196616 | tf_op jit(solution)/shard_map/ppermute | solution.py:34
  29.9 6.9 %collective-permute-start.4 = (bf16[256,128]{1,0:T(8,128)(2,1)S(1)}, bf16[256,128]{1,0:T(8,128)(2,1)S(1)}, u32[]{:S(2)}, u32[]{:S(2)}) collective-permute-start(bf16[256,128]{1,0:T(8,128)(2,1)S(1)} %collective-permute-done.1.r2), channel_id=1, source_target_pairs={{0,1},{1,0},{2,3},{3,2},{4,5},{5,4},{6,7},{7,6},{8,9},{9,8},{10,11... | collective-permute-start | bytes 196616 | tf_op jit(solution)/shard_map/ppermute | solution.py:22
  32.4 4.5 %collective-permute-start.3 = (bf16[256,128]{1,0:T(8,128)(2,1)S(1)}, bf16[256,128]{1,0:T(8,128)(2,1)S(1)}, u32[]{:S(2)}, u32[]{:S(2)}) collective-permute-start(bf16[256,128]{1,0:T(8,128)(2,1)S(1)} %collective-permute-done.r1), channel_id=1, source_target_pairs={{0,1},{1,0},{2,3},{3,2},{4,5},{5,4},{6,7},{7,6},{8,9},{9,8},{10,11... | collective-permute-start | bytes 196616 | tf_op jit(solution)/shard_map/ppermute | solution.py:22
  32.4 4.5 %collective-permute-start.5 = (bf16[256,128]{1,0:T(8,128)(2,1)S(1)}, bf16[256,128]{1,0:T(8,128)(2,1)S(1)}, u32[]{:S(2)}, u32[]{:S(2)}) collective-permute-start(bf16[256,128]{1,0:T(8,128)(2,1)S(1)} %collective-permute-done.2.r3), channel_id=1, source_target_pairs={{0,1},{1,0},{2,3},{3,2},{4,5},{5,4},{6,7},{7,6},{8,9},{9,8},{10,11... | collective-permute-start | bytes 196616 | tf_op jit(solution)/shard_map/ppermute | solution.py:22
  36.8 3.5 %collective-permute-start.15 = (f32[256,128]{1,0:T(8,128)S(1)}, f32[256,128]{1,0:T(8,128)S(1)}, u32[]{:S(2)}, u32[]{:S(2)}) collective-permute-start(f32[256,128]{1,0:T(8,128)S(1)} %get-tuple-element.33), channel_id=1, source_target_pairs={{0,1},{1,0},{2,3},{3,2},{4,5},{5,4},{6,7},{7,6},{8,9},{9,8},{10,11... | collective-permute-start | bytes 393224 | tf_op jit(solution)/shard_map/ppermute | solution.py:22
  39.7 14.1 %collective-permute-start.6 = (f32[3,256,128]{2,1,0:T(8,128)S(1)}, f32[3,256,128]{2,1,0:T(8,128)S(1)}, u32[]{:S(2)}, u32[]{:S(2)}) collective-permute-start(f32[3,256,128]{2,1,0:T(8,128)S(1)} %get-tuple-element.26), channel_id=1, source_target_pairs={{0,1},{1,0},{2,3},{3,2},{4,5},{5,4},{6,7},{7,6},{8,9},{9,8},{10,11... | collective-permute-start | bytes 1179656 | tf_op jit(solution)/shard_map/ppermute | solution.py:22
  40.3 11.6 %collective-permute-start.18 = (bf16[256,128]{1,0:T(8,128)(2,1)S(1)}, bf16[256,128]{1,0:T(8,128)(2,1)S(1)}, u32[]{:S(2)}, u32[]{:S(2)}) collective-permute-start(bf16[256,128]{1,0:T(8,128)(2,1)S(1)} %add_convert_fusion.1.value_ref), channel_id=1, source_target_pairs={{0,6},{2,8},{4,10},{6,12},{8,14},{7,1},{9,3},{11,5},{13,7},{15,9},... | collective-permute-start | bytes 196616 | tf_op jit(solution)/shard_map/ppermute | solution.py:34
  45.9 6.1 %collective-permute-start.17 = (bf16[256,128]{1,0:T(8,128)(2,1)S(1)}, bf16[256,128]{1,0:T(8,128)(2,1)S(1)}, u32[]{:S(2)}, u32[]{:S(2)}) collective-permute-start(bf16[256,128]{1,0:T(8,128)(2,1)S(1)} %add_convert_fusion.1.value_ref), channel_id=1, source_target_pairs={{0,4},{2,6},{4,8},{6,10},{8,12},{10,14},{5,1},{7,3},{9,5},{11,7},{... | collective-permute-start | bytes 196616 | tf_op jit(solution)/shard_map/ppermute | solution.py:34
  47.8 6.0 %collective-permute-start.16 = (bf16[256,128]{1,0:T(8,128)(2,1)S(1)}, bf16[256,128]{1,0:T(8,128)(2,1)S(1)}, u32[]{:S(2)}, u32[]{:S(2)}) collective-permute-start(bf16[256,128]{1,0:T(8,128)(2,1)S(1)} %add_convert_fusion.1.value_ref), channel_id=1, source_target_pairs={{0,2},{2,4},{4,6},{6,8},{8,10},{10,12},{12,14},{3,1},{5,3},{7,5},{... | collective-permute-start | bytes 196616 | tf_op jit(solution)/shard_map/ppermute | solution.py:34
  51.9 4.5 %collective-permute-start.21 = (bf16[256,128]{1,0:T(8,128)(2,1)S(1)}, bf16[256,128]{1,0:T(8,128)(2,1)S(1)}, u32[]{:S(2)}, u32[]{:S(2)}) collective-permute-start(bf16[256,128]{1,0:T(8,128)(2,1)S(1)} %collective-permute-done.18.r3), channel_id=1, source_target_pairs={{0,1},{1,0},{2,3},{3,2},{4,5},{5,4},{6,7},{7,6},{8,9},{9,8},{10,11... | collective-permute-start | bytes 196616 | tf_op jit(solution)/shard_map/ppermute | solution.py:22
  52.0 5.8 %collective-permute-start.20 = (bf16[256,128]{1,0:T(8,128)(2,1)S(1)}, bf16[256,128]{1,0:T(8,128)(2,1)S(1)}, u32[]{:S(2)}, u32[]{:S(2)}) collective-permute-start(bf16[256,128]{1,0:T(8,128)(2,1)S(1)} %collective-permute-done.17.r2), channel_id=1, source_target_pairs={{0,1},{1,0},{2,3},{3,2},{4,5},{5,4},{6,7},{7,6},{8,9},{9,8},{10,11... | collective-permute-start | bytes 196616 | tf_op jit(solution)/shard_map/ppermute | solution.py:22
  53.8 4.0 %collective-permute-start.19 = (bf16[256,128]{1,0:T(8,128)(2,1)S(1)}, bf16[256,128]{1,0:T(8,128)(2,1)S(1)}, u32[]{:S(2)}, u32[]{:S(2)}) collective-permute-start(bf16[256,128]{1,0:T(8,128)(2,1)S(1)} %collective-permute-done.16.r1), channel_id=1, source_target_pairs={{0,1},{1,0},{2,3},{3,2},{4,5},{5,4},{6,7},{7,6},{8,9},{9,8},{10,11... | collective-permute-start | bytes 196616 | tf_op jit(solution)/shard_map/ppermute | solution.py:22
  53.8 13.5 %collective-permute-start.7 = (bf16[256,128]{1,0:T(8,128)(2,1)S(1)}, bf16[256,128]{1,0:T(8,128)(2,1)S(1)}, u32[]{:S(2)}, u32[]{:S(2)}) collective-permute-start(bf16[256,128]{1,0:T(8,128)(2,1)S(1)} %get-tuple-element.47), channel_id=1, source_target_pairs={{2,0},{4,2},{6,4},{8,6},{10,8},{12,10},{14,12},{1,3},{3,5},{5,7},{... | collective-permute-start | bytes 196616 | tf_op jit(solution)/shard_map/ppermute | solution.py:41
  55.1 12.2 %collective-permute-start.9 = (bf16[256,128]{1,0:T(8,128)(2,1)S(1)}, bf16[256,128]{1,0:T(8,128)(2,1)S(1)}, u32[]{:S(2)}, u32[]{:S(2)}) collective-permute-start(bf16[256,128]{1,0:T(8,128)(2,1)S(1)} %get-tuple-element.48), channel_id=1, source_target_pairs={{6,0},{8,2},{10,4},{12,6},{14,8},{1,7},{3,9},{5,11},{7,13},{9,15},... | collective-permute-start | bytes 196616 | tf_op jit(solution)/shard_map/ppermute | solution.py:41
  56.5 10.9 %collective-permute-start.8 = (bf16[256,128]{1,0:T(8,128)(2,1)S(1)}, bf16[256,128]{1,0:T(8,128)(2,1)S(1)}, u32[]{:S(2)}, u32[]{:S(2)}) collective-permute-start(bf16[256,128]{1,0:T(8,128)(2,1)S(1)} %get-tuple-element.49), channel_id=1, source_target_pairs={{4,0},{6,2},{8,4},{10,6},{12,8},{14,10},{1,5},{3,7},{5,9},{7,11},{... | collective-permute-start | bytes 196616 | tf_op jit(solution)/shard_map/ppermute | solution.py:41
  60.8 13.4 %collective-permute-start.22 = (f32[3,256,128]{2,1,0:T(8,128)S(1)}, f32[3,256,128]{2,1,0:T(8,128)S(1)}, u32[]{:S(2)}, u32[]{:S(2)}) collective-permute-start(f32[3,256,128]{2,1,0:T(8,128)S(1)} %get-tuple-element.37), channel_id=1, source_target_pairs={{0,1},{1,0},{2,3},{3,2},{4,5},{5,4},{6,7},{7,6},{8,9},{9,8},{10,11... | collective-permute-start | bytes 1179656 | tf_op jit(solution)/shard_map/ppermute | solution.py:22
  67.4 1.5 %collective-permute-start.10 = (f32[256,128]{1,0:T(8,128)S(1)}, f32[256,128]{1,0:T(8,128)S(1)}, u32[]{:S(2)}, u32[]{:S(2)}) collective-permute-start(f32[256,128]{1,0:T(8,128)S(1)} %convert_add_fusion.1.a_ref), channel_id=1, source_target_pairs={{0,1},{1,0},{2,3},{3,2},{4,5},{5,4},{6,7},{7,6},{8,9},{9,8},{10,11... | collective-permute-start | bytes 393224 | tf_op jit(solution)/shard_map/ppermute | solution.py:22
  71.2 16.7 %collective-permute-start.27 = (bf16[4,16,4096]{2,1,0:T(8,128)(2,1)S(1)}, bf16[4,16,4096]{2,1,0:T(8,128)(2,1)S(1)}, u32[]{:S(2)}, u32[]{:S(2)}) collective-permute-start(bf16[4,16,4096]{2,1,0:T(8,128)(2,1)S(1)} %get-tuple-element.39), channel_id=1, source_target_pairs={{0,2},{2,0},{4,6},{6,4},{8,10},{10,8},{12,14},{14,12},{1,3},{3,1},... | collective-permute-start | bytes 1572872 | tf_op jit(solution)/shard_map/ppermute | solution.py:27
  74.3 18.8 %collective-permute-start.23 = (bf16[256,128]{1,0:T(8,128)(2,1)S(1)}, bf16[256,128]{1,0:T(8,128)(2,1)S(1)}, u32[]{:S(2)}, u32[]{:S(2)}) collective-permute-start(bf16[256,128]{1,0:T(8,128)(2,1)S(1)} %get-tuple-element.44), channel_id=1, source_target_pairs={{2,0},{4,2},{6,4},{8,6},{10,8},{12,10},{14,12},{1,3},{3,5},{5,7},{... | collective-permute-start | bytes 196616 | tf_op jit(solution)/shard_map/ppermute | solution.py:41
  75.6 17.6 %collective-permute-start.25 = (bf16[256,128]{1,0:T(8,128)(2,1)S(1)}, bf16[256,128]{1,0:T(8,128)(2,1)S(1)}, u32[]{:S(2)}, u32[]{:S(2)}) collective-permute-start(bf16[256,128]{1,0:T(8,128)(2,1)S(1)} %get-tuple-element.45), channel_id=1, source_target_pairs={{6,0},{8,2},{10,4},{12,6},{14,8},{1,7},{3,9},{5,11},{7,13},{9,15},... | collective-permute-start | bytes 196616 | tf_op jit(solution)/shard_map/ppermute | solution.py:41
  76.9 16.3 %collective-permute-start.24 = (bf16[256,128]{1,0:T(8,128)(2,1)S(1)}, bf16[256,128]{1,0:T(8,128)(2,1)S(1)}, u32[]{:S(2)}, u32[]{:S(2)}) collective-permute-start(bf16[256,128]{1,0:T(8,128)(2,1)S(1)} %get-tuple-element.46), channel_id=1, source_target_pairs={{4,0},{6,2},{8,4},{10,6},{12,8},{14,10},{1,5},{3,7},{5,9},{7,11},{... | collective-permute-start | bytes 196616 | tf_op jit(solution)/shard_map/ppermute | solution.py:41
  88.6 6.6 %collective-permute-start.28 = (bf16[16,4096]{1,0:T(8,128)(2,1)S(1)}, bf16[16,4096]{1,0:T(8,128)(2,1)S(1)}, u32[]{:S(2)}, u32[]{:S(2)}) collective-permute-start(bf16[16,4096]{1,0:T(8,128)(2,1)S(1)} %get-tuple-element.41), channel_id=1, source_target_pairs={{0,4},{2,6},{4,0},{6,2},{8,12},{10,14},{12,8},{14,10},{1,5},{3,7},... | collective-permute-start | bytes 393224 | tf_op jit(solution)/shard_map/ppermute | solution.py:27
  89.7 13.4 %collective-permute-start.29 = (bf16[16,4096]{1,0:T(8,128)(2,1)S(1)}, bf16[16,4096]{1,0:T(8,128)(2,1)S(1)}, u32[]{:S(2)}, u32[]{:S(2)}) collective-permute-start(bf16[16,4096]{1,0:T(8,128)(2,1)S(1)} %get-tuple-element.42), channel_id=1, source_target_pairs={{0,8},{2,10},{4,12},{6,14},{8,0},{10,2},{12,4},{14,6},{1,9},{3,11}... | collective-permute-start | bytes 393224 | tf_op jit(solution)/shard_map/ppermute | solution.py:27
  93.1 10.0 %collective-permute-start.30 = (bf16[16,4096]{1,0:T(8,128)(2,1)S(1)}, bf16[16,4096]{1,0:T(8,128)(2,1)S(1)}, u32[]{:S(2)}, u32[]{:S(2)}) collective-permute-start(bf16[16,4096]{1,0:T(8,128)(2,1)S(1)} %get-tuple-element.43), channel_id=1, source_target_pairs={{0,12},{2,14},{4,8},{6,10},{8,4},{10,6},{12,0},{14,2},{1,13},{3,15... | collective-permute-start | bytes 393224 | tf_op jit(solution)/shard_map/ppermute | solution.py:27
  93.3 10.6 %collective-permute-start.26 = (f32[256,128]{1,0:T(8,128)S(1)}, f32[256,128]{1,0:T(8,128)S(1)}, u32[]{:S(2)}, u32[]{:S(2)}) collective-permute-start(f32[256,128]{1,0:T(8,128)S(1)} %convert_add_fusion), channel_id=1, source_target_pairs={{0,1},{1,0},{2,3},{3,2},{4,5},{5,4},{6,7},{7,6},{8,9},{9,8},{10,11... | collective-permute-start | bytes 393224 | tf_op jit(solution)/shard_map/ppermute | solution.py:22
  (7 other events, 93.0 us)
